TPU v7x, 256 devices: a whole 4x4x8 slice. The times are simulated.
256 devices in a mesh: vocab: 64 (over x, y_lo, z), dp: 4 (over y_hi, core).
Axes of the slice: x: 4, y: 4 (y_hi: 2, y_lo: 2; y = y_hi * 2 + y_lo), z: 8, core: 2. Of those that a mesh axis runs over, the one named last changes fastest.
Arguments:
- hidden: bfloat16 [1024, 4096], P('dp', 'vocab'), may hold values from -6 to 6
- head_weight: bfloat16 [77824, 4096], P('vocab'), may hold values from -16 to 16
- teacher_codes: int32 [1024, 77824], P('dp', 'vocab'), may hold values from 1 to 126, as said below
- teacher_scales: int32 [1024, 2432], P('dp', 'vocab'), may hold values from -18 to -9
- loss_cotangent: float32 [1024], P('dp'), may hold values from 0.5 to 5
Outputs:
- hidden_grad: bfloat16 [1024, 4096], P('dp', 'vocab')
- head_grad: bfloat16 [77824, 4096], P('vocab', 'dp')
Inputs may be any that keep to these rules, and one draw needn't show every extreme that they name: `teacher_codes`: the sign bit is never set.
All inputs are finite; a program needn't handle non-finite values.
Results may differ from a plain program's by a relative error of at most 0.007.
Values may be sent and summed in bfloat16 or wider, within the bound.
A program may use at most 128 MiB of HBM per device.

v0:
```python
import jax
import jax.numpy as jnp
from jax import lax
from jax.sharding import PartitionSpec as P


def decode_teacher(codes, scales):
    field = codes // 8
    mantissa = (codes % 8).astype(jnp.float32)
    normal_value = (8.0 + mantissa) * jnp.exp2((field - 10).astype(jnp.float32))
    tiny_value = mantissa * 2.0 ** (-9)
    value = jnp.where(field == 0, tiny_value, normal_value)
    rows, width = codes.shape
    blocks = value.reshape(rows, width // 32, 32) * jnp.exp2(scales.astype(jnp.float32))[:, :, None]
    return blocks.reshape(rows, width)


def per_device(hidden, head_weight, teacher_codes, teacher_scales, loss_cotangent):
    piece = lax.all_gather(hidden, "vocab", axis=1, tiled=True)
    columns = head_weight
    logits = lax.dot_general(
        piece, columns, (((1,), (1,)), ((), ())), preferred_element_type=jnp.float32
    )
    gathered = piece
    logits, gathered = (logits, gathered)
    teacher = decode_teacher(teacher_codes, teacher_scales)
    local_max = jnp.max(logits, axis=1)
    local_teacher = jnp.sum(teacher, axis=1)
    row_max = lax.pmax(local_max, "vocab")
    shifted = jnp.exp(logits - row_max[:, None])
    local_sum = jnp.sum(shifted, axis=1)
    row_sum, teacher_total = lax.psum((local_sum, local_teacher), "vocab")
    probs = shifted / row_sum[:, None]
    token_grad = (loss_cotangent[:, None] * (probs - teacher / teacher_total[:, None])).astype(
        jnp.bfloat16
    )
    columns = head_weight
    transposed = lax.psum_scatter(
        lax.dot_general(
            columns, token_grad, (((0,), (1,)), ((), ())), preferred_element_type=jnp.float32
        ),
        "vocab",
        scatter_dimension=0,
        tiled=True,
    )
    hidden_grad = transposed.T.astype(jnp.bfloat16)
    quarters = lax.all_to_all(gathered, "dp", split_axis=1, concat_axis=0, tiled=True)
    head_grad = lax.dot_general(
        lax.all_gather(token_grad, "dp", axis=0, tiled=True),
        quarters,
        (((0,), (0,)), ((), ())),
        preferred_element_type=jnp.float32,
    ).astype(jnp.bfloat16)
    return (hidden_grad, head_grad)


def solution(mesh):
    return jax.shard_map(
        per_device,
        mesh=mesh,
        in_specs=(P("dp", "vocab"), P("vocab", None), P("dp", "vocab"), P("dp", "vocab"), P("dp")),
        out_specs=(P("dp", "vocab"), P("vocab", "dp")),
        check_vma=False,
    )
```

profile of v0, /device:TPU:16, one launch (start us, length us, event | category | flops | bytes accessed | tf_op | source)
XLA Modules:
  0.0 1003.1 jit_solution(2723529928922365066)
XLA Ops:
  7.2 0.0 all-gather.3.cloned.1.call-start
  7.2 0.7 all-gather.3.cloned.1.call-update
  7.9 0.0 all-gather.5.cloned.1.call-start
  7.9 0.8 multiply_exponential_fusion
  8.7 2.9 fusion.3
  11.6 300.5 %all-gather.3.cloned.1.call-done = bf16[256,4096]{0,1:T(8,128)(2,1)} async-done(((bf16[256,64]{0,1:T(8,128)(2,1)}), bf16[256,4096]{0,1:T(8,128)(2,1)}) %all-gather.3.cloned.1.call-update) | async-done | bytes 2097168 | tf_op jit(solution)/shard_map/all_gather | solution.py:19
  312.1 6.1 fusion.4
  318.2 0.0 copy-start
  318.2 0.0 copy-start.1
  318.2 157.4 %pmax.7 = f32[256]{0:T(256)S(1)} all-reduce(f32[256]{0:T(256)S(1)} %get-tuple-element.12), channel_id=1, replica_groups=mesh['vocab'=64,'dp'=4] {'vocab'}, use_global_device_ids=true, to_apply=%region_1.2 | all-reduce | flops 256 | bytes 2048 | tf_op jit(solution)/shard_map/pmax | solution.py:29
  475.6 0.3 fusion.2
  475.8 152.3 %all-reduce = (f32[256]{0:T(256)S(1)}, f32[256]{0:T(256)S(1)}) all-reduce(f32[256]{0:T(256)S(1)} %fusion.3, f32[256]{0:T(256)S(1)} %fusion.2), channel_id=1, replica_groups=mesh['vocab'=64,'dp'=4] {'vocab'}, use_global_device_ids=true, to_apply=%region_5.6 | all-reduce | flops 512 | bytes 4096 | tf_op jit(solution)/shard_map/psum | solution.py:32
  628.2 2.7 multiply_convert_fusion
  630.8 0.0 all-gather.5.cloned.1.call-update
  630.9 0.0 reduce-scatter.4.cloned.1.call-start
  630.9 8.9 convolution_bitcast_fusion
  639.8 5.6 copy.13
  645.5 0.0 reduce-scatter.4.cloned.1.call-update
  645.5 30.3 %all_to_all.19 = bf16[256,4,1024]{0,2,1:T(8,128)(2,1)S(1)} all-to-all(bf16[256,4,1024]{0,2,1:T(8,128)(2,1)} %bitcast.22), channel_id=1, replica_groups=mesh['vocab'=64,'dp'=4] {'dp'}, dimensions={1} | all-to-all | bytes 4194304 | tf_op jit(solution)/shard_map/all_to_all | solution.py:47
  675.8 2.5 copy.11
  678.3 6.5 convolution_convert_fusion
  684.8 310.0 %reduce-scatter.4.cloned.1.call-done = f32[64,256]{1,0:T(8,128)} async-done(((f32[4096,256]{1,0:T(8,128)}), f32[64,256]{1,0:T(8,128)}) %reduce-scatter.4.cloned.1.call-update) | async-done | bytes 65552
  994.9 0.9 copy.14
  995.8 0.7 copy.12
  (3 shorter events, 0.0 us)
Async XLA Ops:
  7.2 305.0 %all-gather.3.cloned.1.call-start = ((), (), s32[]{:S(2)}) async-start(), calls=%async_computation.2 | async-start | bytes 2129920 | tf_op jit(solution)/shard_map/all_gather | solution.py:19
  7.9 670.4 %all-gather.5.cloned.1.call-start = ((), (), s32[]{:S(2)}) async-start(), calls=%async_computation.3 | async-start | bytes 3112960 | tf_op jit(solution)/shard_map/all_gather | solution.py:49
  318.2 310.0 %copy-start = (s32[256,1216]{0,1:T(8,128)S(1)}, s32[256,1216]{0,1:T(8,128)}, u32[]{:S(2)}) copy-start(s32[256,1216]{0,1:T(8,128)} %param.7) | copy-start | bytes 3735556
  318.2 310.0 %copy-start.1 = (f32[256]{0:T(256)S(1)}, f32[256]{0:T(256)}, u32[]{:S(2)}) copy-start(f32[256]{0:T(256)} %param.9) | copy-start | bytes 3076
  630.9 364.0 %reduce-scatter.4.cloned.1.call-start = ((), (), s32[]{:S(2)}) async-start(), calls=%async_computation.4 | async-start | bytes 4259840
Sparse Core Ops, SparseCore 0:
  9.8 302.2 all-gather.2
  631.0 26.3 all-gather.4
  659.9 334.9 reduce-scatter.3
where the time goes:
time: 1000 us
  waiting for transfers between devices  611 us (61%)
  blocking collectives  340 us (34%)
  matrix products  21.6 us (2%)
  between operations  13.8 us (1%)
    unnamed x4, waiting for transfers between devices  311 us
    all_gather x1, waiting for transfers between devices, per_device(): piece = lax.all_gather(hidden, 'vocab', axis=1, tiled=True)  300 us
    pmax x1, blocking collectives, per_device(): row_max = lax.pmax(local_max, 'vocab')  157 us
    psum x1, blocking collectives, per_device(): row_sum, teacher_total = lax.psum((local_sum, local_teacher), 'vocab')  152 us
    all_to_all x1, blocking collectives, per_device(): lax.all_to_all(gathered, 'dp', split_axis=1, concat_axis=0, tiled=True)  30.3 us
  transfers between devices with their start and end apart: 3, of which 2 were waited for; matrix products, arithmetic and copies ran while one was open for 3% of the time, Pallas kernels for 0%

commit v1 on v0

v1 whole, which is shorter than its diff:
```python
import jax
import jax.numpy as jnp
from jax import lax
from jax.experimental import pallas as pl
from jax.experimental.pallas import tpu as pltpu
from jax.sharding import PartitionSpec as P

BF = jnp.bfloat16
F32 = jnp.float32
MESH = pl.DeviceIdType.MESH

V = 1216
T = 256
NEAR = (0, 1, 7, 2, 6, 3, 5, 4)
FAR = (4, 3, 5, 2, 6, 1, 7, 0)


def rows(start, size):
    return pl.ds(pl.multiple_of(start, size), size)


def kernel(
    hid,
    scales,
    cot,
    w_hbm,
    codes_hbm,
    hg_out,
    head_out,
    h,
    w,
    codes,
    teach,
    logits,
    tg,
    tg_all,
    hx_all,
    part,
    rx,
    acc,
    qy,
    ry,
    qz,
    rz,
    st,
    st_z,
    st_xy,
    out,
    local_sem,
    out_sem,
    ag_send_z,
    ag_send_y,
    ag_send_x,
    ag_send_x2,
    ag_recv,
    hx_send,
    hx_recv,
    tg_send,
    tg_recv,
    st_send,
    st_recv,
    rs_send,
    rs_recv,
    rp_send,
    rp_recv,
    ry_send,
    ry_recv,
    rz_send,
    rz_recv,
):
    v = lax.axis_index("vocab")
    d = lax.axis_index("dp")
    x, y, z = v // 16, (v // 8) % 2, v % 8
    yh, core = d // 2, d % 2

    def at(dx, dy, dz):
        return ((x + dx) % 4 * 2 + (y + dy) % 2) * 8 + (z + dz) % 8

    def dev(dx, dy, dz):
        return (at(dx, dy, dz), d)

    other = (1 - yh) * 2
    cross = [(at(0, 1, 0), other), (at(0, 1, 0), other + 1)]
    twin = (v, yh * 2 + 1 - core)
    opposite = (v, other + core)

    def remote(src, dst, ss, rs, to):
        return pltpu.make_async_remote_copy(
            src_ref=src, dst_ref=dst, send_sem=ss, recv_sem=rs, device_id=to, device_id_type=MESH
        )

    def arrived(ref, rs):
        remote(ref, ref, local_sem.at[0], rs, twin).wait_recv()

    def sent(ref, ss):
        remote(ref, ref, ss, local_sem.at[0], twin).wait_send()

    barrier = pltpu.get_barrier_semaphore()
    partners = [dev(0, 0, dz) for dz in range(1, 8)]
    partners += [dev(dx, dy, 0) for dx in range(4) for dy in range(2) if dx or dy]
    partners += cross + [twin, opposite]
    for p in partners:
        pl.semaphore_signal(barrier, inc=1, device_id=p, device_id_type=MESH)

    codes_copy = pltpu.make_async_copy(codes_hbm, codes, local_sem.at[1])
    codes_copy.start()
    w_copy = pltpu.make_async_copy(w_hbm, w, local_sem.at[2])
    w_copy.start()

    h[rows(v * 64, 64), :] = hid[...]

    codes_copy.wait()

    def decode(b, total):
        r = rows(b * 32, 32)
        c = codes[r, :]
        field = c >> 3
        mantissa = (c & 7).astype(F32)
        s = scales[pl.ds(b, 1), :]
        digits = jnp.where(field == 0, 2.0 * mantissa, 8.0 + mantissa)
        value = digits * jnp.exp2((field - 10 + s).astype(F32))
        teach[r, :] = value
        return total + value

    total = lax.fori_loop(0, V // 32, decode, jnp.zeros((32, T), F32))
    teacher_sum = jnp.sum(total, axis=0, keepdims=True)

    pl.semaphore_wait(barrier, len(partners))

    def block(dx, dy, k):
        return h.at[rows(at(dx, dy, -NEAR[k]) * 64, 64), :]

    def spread_x(dy, k):
        for i, dx in ((0, 1), (1, -1)):
            b = block(0, dy, k)
            remote(b, b, ag_send_x.at[i, dy, k], ag_recv.at[1 + i, dy, k], dev(dx, 0, 0)).start()

    def spread_y(k):
        b = block(0, 0, k)
        remote(b, b, ag_send_y.at[k], ag_recv.at[0, 1, k], dev(0, 1, 0)).start()

    mine = block(0, 0, 0)
    for k in range(1, 8):
        remote(mine, mine, ag_send_z.at[k], ag_recv.at[0, 0, k], dev(0, 0, NEAR[k])).start()
    for k in range(8):
        if k:
            arrived(block(0, 0, k), ag_recv.at[0, 0, k])
        spread_x(0, k)
        spread_y(k)
    for k in range(8):
        arrived(block(0, 1, k), ag_recv.at[0, 1, k])
        spread_x(1, k)

    def chunk(dx, dy):
        return ((x + dx) % 4 * 2 + (y + dy) % 2) * 512

    def add_logits(start):
        f = rows(start, 512)
        logits[...] += jnp.dot(w[:, f], h[f, :], preferred_element_type=F32)

    logits[...] = jnp.zeros_like(logits)
    w_copy.wait()

    def dots_0(i, _):
        add_logits(chunk(0, i))
        return 0

    lax.fori_loop(0, 2, dots_0, 0)
    for dy in range(2):
        for k in range(8):
            for i, dx in ((0, 1), (1, -1)):
                b = block(-dx, dy, k)
                arrived(b, ag_recv.at[1 + i, dy, k])
                if k % 2 == i:
                    remote(b, b, ag_send_x2.at[dy, k], ag_recv.at[3, dy, k], dev(dx, 0, 0)).start()

    def dots_1(i, _):
        add_logits(chunk(1 + i // 2 * 2, i % 2))
        return 0

    lax.fori_loop(0, 4, dots_1, 0)
    for dy in range(2):
        for k in range(8):
            arrived(block(2, dy, k), ag_recv.at[3, dy, k])

    own_lanes = rows(d * T, T)
    for c2 in range(2):
        src = h.at[rows(((other + c2) * 2 + y) * 512, 512), :]
        dst = hx_all.at[rows(y * 512, 512), own_lanes]
        remote(src, dst, hx_send.at[c2], hx_recv.at[core], cross[c2]).start()
    src = h.at[rows((yh * 2 + 1 - core) * 1024, 1024), :]
    remote(src, hx_all.at[:, own_lanes], hx_send.at[2], hx_recv.at[2], twin).start()
    hx_all[:, own_lanes] = h[rows(d * 1024, 1024), :]

    def dots_2(i, _):
        add_logits(chunk(2, i))
        return 0

    lax.fori_loop(0, 2, dots_2, 0)

    def top(b, m):
        return jnp.maximum(m, logits[rows(b * 32, 32), :])

    m = lax.fori_loop(1, V // 32, top, logits[0:32, :])
    local_max = jnp.max(m, axis=0, keepdims=True)

    def exps(b, s):
        r = rows(b * 32, 32)
        e = jnp.exp(logits[r, :] - local_max)
        logits[r, :] = e
        return s + e

    s = lax.fori_loop(0, V // 32, exps, jnp.zeros((32, T), F32))
    local_sum = jnp.sum(s, axis=0, keepdims=True)

    def share(m, s, t, stage, buf, peers):
        st[stage, 0:1, :] = m
        st[stage, 1:2, :] = s
        st[stage, 2:3, :] = t
        for j, p in enumerate(peers):
            remote(st.at[stage], buf.at[j], st_send.at[stage, j], st_recv.at[stage, j], p).start()
        for j in range(7):
            arrived(buf.at[j], st_recv.at[stage, j])
        best = m
        for j in range(7):
            best = jnp.maximum(best, buf[j, 0:1, :])
        s = s * jnp.exp(m - best)
        for j in range(7):
            s += buf[j, 1:2, :] * jnp.exp(buf[j, 0:1, :] - best)
            t += buf[j, 2:3, :]
        return best, s, t

    st[...] = jnp.zeros_like(st)
    along_z = [dev(0, 0, dz) for dz in FAR[:7]]
    along_xy = [dev(dx, dy, 0) for dx, dy in ((2, 1), (2, 0), (1, 1), (3, 1), (1, 0), (3, 0), (0, 1))]
    row_max, row_sum, row_teach = share(local_max, local_sum, teacher_sum, 0, st_z, along_z)
    row_max, row_sum, row_teach = share(row_max, row_sum, row_teach, 1, st_xy, along_xy)

    up = cot[...] * jnp.exp(local_max - row_max) / row_sum
    down = cot[...] / row_teach

    def grads(b, _):
        r = rows(b * 32, 32)
        g = (logits[r, :] * up - teach[r, :] * down).astype(BF)
        tg[r, :] = g
        tg_all[r, own_lanes] = g
        return 0

    lax.fori_loop(0, V // 32, grads, 0)

    remote(tg, tg_all.at[:, own_lanes], tg_send.at[0], tg_recv.at[0], opposite).start()
    remote(tg, tg_all.at[:, own_lanes], tg_send.at[1], tg_recv.at[1], twin).start()

    def dot_chunk(start):
        return lax.dot_general(
            w[:, rows(start, 512)], tg[...], (((0,), (0,)), ((), ())), preferred_element_type=F32
        )

    def direct(i, _):
        way, slot = i % 2, i // 2
        start = chunk(2 - slot + 2 * slot * way, way + slot)
        f = rows(start, 512)
        part[f, :] = dot_chunk(start).astype(BF)
        to = dev(1 - 2 * way, 0, 0)
        remote(part.at[f, :], rx.at[way, slot], rs_send.at[way, slot], rs_recv.at[way, slot], to).start()
        return 0

    lax.fori_loop(0, 4, direct, 0)

    theirs = pl.ds(pl.multiple_of(other * T, 2 * T), 2 * T)
    for c2 in range(2):
        arrived(hx_all.at[rows((1 - y) * 512, 512), own_lanes], hx_recv.at[c2])
    src = hx_all.at[rows((1 - y) * 512, 512), theirs]
    remote(src, src, hx_send.at[3], hx_recv.at[3], dev(0, 1, 0)).start()

    def combined(way, _):
        start = chunk(1 + 2 * way, way)
        f = rows(start, 512)
        arrived(rx.at[way, 0], rs_recv.at[way, 0])
        part[f, :] = (dot_chunk(start) + rx[way, 0].astype(F32)).astype(BF)
        to = dev(1 - 2 * way, 0, 0)
        for k in range(8):
            zz = (z + FAR[k]) % 8
            src = part.at[rows(start + zz * 64, 64), :]
            dst = rx.at[way, 2, rows(zz * 64, 64), :]
            remote(src, dst, rp_send.at[way, k], rp_recv.at[way, k], to).start()
        return 0

    lax.fori_loop(0, 2, combined, 0)

    def own(dy, _):
        acc[dy] = dot_chunk(chunk(0, dy))
        return 0

    lax.fori_loop(0, 2, own, 0)
    for way in range(2):
        arrived(rx.at[way, 1], rs_recv.at[way, 1])
        acc[1 - way] += rx[way, 1].astype(F32)

    def finish_y(k):
        zz = (z + FAR[k]) % 8
        r = rows(zz * 64, 64)
        for way in (1, 0):
            arrived(rx.at[way, 2, r, :], rp_recv.at[way, k])
            total = acc[way, r, :] + rx[way, 2, r, :].astype(F32)
            if way:
                qy[r, :] = total.astype(BF)
                src = qy.at[r, :]
                remote(src, ry.at[r, :], ry_send.at[k], ry_recv.at[k], dev(0, 1, 0)).start()
            else:
                acc[0, r, :] = total

    def finish_z(k):
        zz = (z + FAR[k]) % 8
        r = rows(zz * 64, 64)
        arrived(ry.at[r, :], ry_recv.at[k])
        total = acc[0, r, :] + ry[r, :].astype(F32)
        if k == 7:
            return total
        qz[r, :] = total.astype(BF)
        remote(qz.at[r, :], rz.at[k], rz_send.at[k], rz_recv.at[k], dev(0, 0, FAR[k])).start()

    mine = None
    for k in range(9):
        if k < 8:
            finish_y(k)
        if k > 0:
            mine = finish_z(k - 1)
    acc[0, 0:64, :] = mine

    arrived(tg_all.at[:, own_lanes], tg_recv.at[0])
    src = tg_all.at[:, rows((other + core) * T, T)]
    remote(src, src, tg_send.at[2], tg_recv.at[2], twin).start()
    arrived(tg_all.at[:, own_lanes], tg_recv.at[1])
    arrived(hx_all.at[:, own_lanes], hx_recv.at[2])
    arrived(hx_all.at[rows(y * 512, 512), theirs], hx_recv.at[3])
    arrived(tg_all.at[:, own_lanes], tg_recv.at[2])

    def head(i, _):
        r = rows(i * 304, 304)
        out[r, :] = lax.dot_general(
            tg_all[r, :], hx_all[...], (((1,), (1,)), ((), ())), preferred_element_type=F32
        ).astype(BF)
        pltpu.make_async_copy(out.at[r, :], head_out.at[r, :], out_sem.at[i]).start()
        return 0

    lax.fori_loop(0, 4, head, 0)

    total = acc[0, 0:64, :]
    for k in range(7):
        arrived(rz.at[k], rz_recv.at[k])
        total += rz[k].astype(F32)
    hg_out[...] = total.astype(BF)

    for i in range(4):
        r = rows(i * 304, 304)
        pltpu.make_async_copy(out.at[r, :], head_out.at[r, :], out_sem.at[i]).wait()
    one = h.at[0:64, :]
    for k in range(8):
        if k:
            sent(one, ag_send_z.at[k])
        sent(one, ag_send_y.at[k])
        for dy in range(2):
            sent(one, ag_send_x.at[0, dy, k])
            sent(one, ag_send_x.at[1, dy, k])
            sent(one, ag_send_x2.at[dy, k])
    for c2 in range(2):
        sent(h.at[0:512, :], hx_send.at[c2])
    sent(h.at[0:1024, :], hx_send.at[2])
    sent(hx_all.at[rows((1 - y) * 512, 512), theirs], hx_send.at[3])
    for i in range(3):
        sent(tg, tg_send.at[i])
    for i in range(2):
        for j in range(7):
            sent(st.at[i], st_send.at[i, j])
        sent(rx.at[i, 0], rs_send.at[i, 0])
        sent(rx.at[i, 1], rs_send.at[i, 1])
        for k in range(8):
            sent(one, rp_send.at[i, k])
    for k in range(8):
        sent(one, ry_send.at[k])
        if k < 7:
            sent(one, rz_send.at[k])


def per_device(hidden, head_weight, teacher_codes, teacher_scales, loss_cotangent):
    dma = pltpu.SemaphoreType.DMA
    vmem = pl.BlockSpec(memory_space=pltpu.VMEM)
    hbm = pl.BlockSpec(memory_space=pl.ANY)
    hidden_grad, head_grad = pl.pallas_call(
        kernel,
        name="head_backward",
        out_shape=(
            jax.ShapeDtypeStruct((64, T), BF),
            jax.ShapeDtypeStruct((V, 1024), BF),
        ),
        in_specs=[vmem, vmem, vmem, hbm, hbm],
        out_specs=(vmem, hbm),
        scratch_shapes=[
            pltpu.VMEM((4096, T), BF),
            pltpu.VMEM((V, 4096), BF),
            pltpu.VMEM((V, T), jnp.int32),
            pltpu.VMEM((V, T), F32),
            pltpu.VMEM((V, T), F32),
            pltpu.VMEM((V, T), BF),
            pltpu.VMEM((V, 4 * T), BF),
            pltpu.VMEM((1024, 4 * T), BF),
            pltpu.VMEM((4096, T), BF),
            pltpu.VMEM((2, 3, 512, T), BF),
            pltpu.VMEM((2, 512, T), F32),
            pltpu.VMEM((512, T), BF),
            pltpu.VMEM((512, T), BF),
            pltpu.VMEM((512, T), BF),
            pltpu.VMEM((7, 64, T), BF),
            pltpu.VMEM((2, 8, T), F32),
            pltpu.VMEM((7, 8, T), F32),
            pltpu.VMEM((7, 8, T), F32),
            pltpu.VMEM((V, 1024), BF),
            dma((3,)),
            dma((4,)),
            dma((8,)),
            dma((8,)),
            dma((2, 2, 8)),
            dma((2, 8)),
            dma((4, 2, 8)),
            dma((4,)),
            dma((4,)),
            dma((3,)),
            dma((3,)),
            dma((2, 7)),
            dma((2, 7)),
            dma((2, 2)),
            dma((2, 2)),
            dma((2, 8)),
            dma((2, 8)),
            dma((8,)),
            dma((8,)),
            dma((8,)),
            dma((8,)),
        ],
        compiler_params=pltpu.CompilerParams(
            collective_id=0, has_side_effects=True, vmem_limit_bytes=56 << 20
        ),
        cost_estimate=pl.CostEstimate(
            flops=6 * V * T * 4096, bytes_accessed=14 << 20, transcendentals=2 * V * T
        ),
    )(hidden.T, teacher_scales.T, loss_cotangent.reshape(1, T), head_weight, teacher_codes.T)
    return hidden_grad.T, head_grad


def solution(mesh):
    return jax.shard_map(
        per_device,
        mesh=mesh,
        in_specs=(P("dp", "vocab"), P("vocab", None), P("dp", "vocab"), P("dp", "vocab"), P("dp")),
        out_specs=(P("dp", "vocab"), P("vocab", "dp")),
        check_vma=False,
    )
```

time: 1000 us -> 90.4 us (0.09)
  the two profiles are of different devices: /device:TPU:16 before, /device:TPU:37 now
where the time goes in v1:
time: 90.4 us; the launch traced here: 90.1 us
  Pallas kernels  84.8 us (94%)
  local copies, waits for them, and re-layouts  4.75 us (5%)
    pallas_call x1, Pallas kernels, per_device(): pl.pallas_call(kernel, name='head_backward', out_shape=(jax.ShapeDtypeStr...  84.8 us
    unnamed x2, local copies, waits for them, and re-layouts  4.75 us

profile of v1, /device:TPU:37, one launch (start us, length us, event | category | flops | bytes accessed | tf_op | source)
XLA Modules:
  0.0 90.1 jit_solution(812879091999895959)
XLA Ops:
  0.6 84.8 %head_backward.1 = (bf16[64,256]{1,0:T(8,128)(2,1)}, bf16[1216,1024]{1,0:T(8,128)(2,1)}) custom-call(bf16[64,256]{1,0:T(8,128)(2,1)} %bitcast.8, s32[38,256]{1,0:T(8,128)} %bitcast.7, f32[1,256]{1,0:T(1,128)} %bitcast.9, bf16[1216,4096]{1,0:T(8,128)(2,1)} %w_hbm.1, s32[1216,256]{1,0:T(8,128)} %bitcast.6), custom_call_target="tpu_custom_call" | custom-call | flops 7650410496 | bytes 14680064 | tf_op jit(solution)/shard_map/head_backward/pallas_call | solution.py:390
  85.4 1.4 %copy.9 = bf16[256,64]{0,1:T(8,128)(2,1)} copy(bf16[256,64]{0,1:T(8,128)(2,1)} %bitcast.5) | data formatting | bytes 65536
  86.8 3.4 %copy.10 = bf16[1216,1024]{1,0:T(8,128)(2,1)} copy(bf16[1216,1024]{1,0:T(8,128)(2,1)} %get-tuple-element.9) | data formatting | bytes 4980736

commit v2 on v1

v2 whole, which is shorter than its diff:
```python
import jax
import jax.numpy as jnp
from jax import lax
from jax.experimental import pallas as pl
from jax.experimental.pallas import tpu as pltpu
from jax.sharding import PartitionSpec as P

BF = jnp.bfloat16
F32 = jnp.float32
MESH = pl.DeviceIdType.MESH

V = 1216
T = 256
NEAR = (0, 1, 7, 2, 6, 3, 5, 4)
FAR = (4, 3, 5, 2, 6, 1, 7, 0)


def rows(start, size):
    return pl.ds(pl.multiple_of(start, size), size)


def kernel(
    hid_hbm,
    scales_hbm,
    cot_hbm,
    w_hbm,
    codes_hbm,
    hg_out,
    head_out,
    scales,
    cot,
    h,
    w,
    codes,
    teach,
    logits,
    tg,
    tg_all,
    hx_all,
    part,
    rx,
    rf,
    qf,
    ro,
    acc,
    qy,
    ry,
    qz,
    rz,
    st,
    st_z,
    st_xy,
    local_sem,
    ag_send_z,
    ag_send_y,
    ag_send_x,
    ag_recv,
    hx_send,
    hx_recv,
    tg_send,
    tg_recv,
    st_send,
    st_recv,
    rs_send,
    rs_recv,
    rf_send,
    rf_recv,
    ro_send,
    ro_recv,
    ry_send,
    ry_recv,
    rz_send,
    rz_recv,
):
    v = lax.axis_index("vocab")
    d = lax.axis_index("dp")
    x, y, z = v // 16, (v // 8) % 2, v % 8
    yh, core = d // 2, d % 2

    def at(dx, dy, dz):
        return ((x + dx) % 4 * 2 + (y + dy) % 2) * 8 + (z + dz) % 8

    def dev(dx, dy, dz):
        return (at(dx, dy, dz), d)

    other = (1 - yh) * 2
    cross = [(at(0, 1, 0), other), (at(0, 1, 0), other + 1)]
    twin = (v, yh * 2 + 1 - core)
    opposite = (v, other + core)

    def remote(src, dst, ss, rs, to):
        return pltpu.make_async_remote_copy(
            src_ref=src, dst_ref=dst, send_sem=ss, recv_sem=rs, device_id=to, device_id_type=MESH
        )

    def arrived(ref, rs):
        remote(ref, ref, local_sem.at[0], rs, twin).wait_recv()

    def sent(ref, ss):
        remote(ref, ref, ss, local_sem.at[0], twin).wait_send()

    barrier = pltpu.get_barrier_semaphore()
    partners = [dev(0, 0, dz) for dz in range(1, 8)]
    partners += [dev(dx, dy, 0) for dx in range(4) for dy in range(2) if dx or dy]
    partners += cross + [twin, opposite]
    for p in partners:
        pl.semaphore_signal(barrier, inc=1, device_id=p, device_id_type=MESH)

    loads = [
        pltpu.make_async_copy(src, dst, local_sem.at[1 + i])
        for i, (src, dst) in enumerate(
            (
                (hid_hbm, h.at[rows(v * 64, 64), :]),
                (scales_hbm, scales),
                (codes_hbm, codes),
                (cot_hbm, cot),
                (w_hbm, w),
            )
        )
    ]
    for load in loads:
        load.start()

    loads[1].wait()
    loads[2].wait()

    def decode(b, total):
        r = rows(b * 32, 32)
        c = codes[r, :]
        field = c >> 3
        mantissa = (c & 7).astype(F32)
        s = scales[pl.ds(b, 1), :]
        digits = jnp.where(field == 0, 2.0 * mantissa, 8.0 + mantissa)
        value = digits * jnp.exp2((field - 10 + s).astype(F32))
        teach[r, :] = value
        return total + value

    total = lax.fori_loop(0, V // 32, decode, jnp.zeros((32, T), F32))
    teacher_sum = jnp.sum(total, axis=0, keepdims=True)

    loads[0].wait()
    loads[3].wait()
    pl.semaphore_wait(barrier, len(partners))

    def block(dx, dy, k):
        return h.at[rows(at(dx, dy, -NEAR[k]) * 64, 64), :]

    def pass_on(b, ss, rs, to):
        remote(b, b, ss, rs, to).start()

    def spread_x(dy, k):
        for i, dx in ((0, 1), (1, -1)):
            pass_on(block(0, dy, k), ag_send_x.at[i, dy, k], ag_recv.at[2 + i, dy, k], dev(dx, 0, 0))

    def spread_y(far, k):
        pass_on(block(2 * far, 0, k), ag_send_y.at[far, k], ag_recv.at[far, 1, k], dev(0, 1, 0))

    def spread_z(far):
        for k in range(1, 8):
            pass_on(block(2 * far, 0, 0), ag_send_z.at[far, k], ag_recv.at[far, 0, k], dev(0, 0, NEAR[k]))

    def chunk(dx, dy):
        return ((x + dx) % 4 * 2 + (y + dy) % 2) * 512

    own_lanes = rows(d * T, T)

    def hidden_across(dx):
        quarter = (x + dx) % 4

        @pl.when(quarter // 2 == 1 - yh)
        def _():
            c2 = quarter % 2
            src = h.at[rows(chunk(dx, 0), 512), :]
            dst = hx_all.at[rows(y * 512, 512), own_lanes]
            to = (at(0, 1, 0), other + c2)
            remote(src, dst, hx_send.at[c2], hx_recv.at[core], to).start()

    pass_on(block(0, 0, 0), ag_send_z.at[0, 0], ag_recv.at[1, 0, 0], dev(2, 0, 0))
    spread_z(0)
    spread_x(0, 0)
    spread_y(0, 0)
    for k in range(1, 8):
        arrived(block(0, 0, k), ag_recv.at[0, 0, k])
        spread_x(0, k)
        spread_y(0, k)
        if k == 2:
            arrived(block(2, 0, 0), ag_recv.at[1, 0, 0])
            spread_z(1)
            spread_y(1, 0)
    hidden_across(0)
    for k in range(8):
        arrived(block(0, 1, k), ag_recv.at[0, 1, k])
        spread_x(1, k)
        if k:
            arrived(block(2, 0, k), ag_recv.at[1, 0, k])
            spread_y(1, k)
    hidden_across(2)

    def add_logits(start):
        f = rows(start, 512)
        logits[...] += jnp.dot(w[:, f], h[f, :], preferred_element_type=F32)

    logits[...] = jnp.zeros_like(logits)
    loads[4].wait()

    def dots_near(i, _):
        add_logits(chunk(0, i))
        return 0

    lax.fori_loop(0, 2, dots_near, 0)
    add_logits(chunk(2, 0))
    for dy in range(2):
        for k in range(8):
            for i, dx in ((0, 1), (1, -1)):
                arrived(block(-dx, dy, k), ag_recv.at[2 + i, dy, k])
        if dy == 0:
            hidden_across(1)
            hidden_across(3)

            def dots_side(i, _):
                add_logits(chunk(1 + 2 * i, 0))
                return 0

            lax.fori_loop(0, 2, dots_side, 0)
    for k in range(8):
        arrived(block(2, 1, k), ag_recv.at[1, 1, k])
    src = h.at[rows((yh * 2 + 1 - core) * 1024, 1024), :]
    remote(src, hx_all.at[:, own_lanes], hx_send.at[2], hx_recv.at[2], twin).start()
    hx_all[:, own_lanes] = h[rows(d * 1024, 1024), :]

    def dots_last(i, _):
        add_logits(chunk(1 + i, 1))
        return 0

    lax.fori_loop(0, 3, dots_last, 0)

    def top(b, m):
        return jnp.maximum(m, logits[rows(b * 32, 32), :])

    m = lax.fori_loop(1, V // 32, top, logits[0:32, :])
    local_max = jnp.max(m, axis=0, keepdims=True)

    def exps(b, s):
        r = rows(b * 32, 32)
        e = jnp.exp(logits[r, :] - local_max)
        logits[r, :] = e
        return s + e

    s = lax.fori_loop(0, V // 32, exps, jnp.zeros((32, T), F32))
    local_sum = jnp.sum(s, axis=0, keepdims=True)

    def hidden_along():
        for c2 in range(2):
            lanes = rows((other + c2) * T, T)
            src = hx_all.at[rows((1 - y) * 512, 512), lanes]
            arrived(src, hx_recv.at[c2])
            remote(src, src, hx_send.at[3 + c2], hx_recv.at[3 + c2], dev(0, 1, 0)).start()

    def share(m, s, t, stage, buf, peers):
        st[stage, 0:1, :] = m
        st[stage, 1:2, :] = s
        st[stage, 2:3, :] = t
        for j, p in enumerate(peers):
            remote(st.at[stage], buf.at[j], st_send.at[stage, j], st_recv.at[stage, j], p).start()
        if stage:
            hidden_along()
        for j in range(7):
            arrived(buf.at[j], st_recv.at[stage, j])
        best = m
        for j in range(7):
            best = jnp.maximum(best, buf[j, 0:1, :])
        s = s * jnp.exp(m - best)
        for j in range(7):
            s += buf[j, 1:2, :] * jnp.exp(buf[j, 0:1, :] - best)
            t += buf[j, 2:3, :]
        return best, s, t

    st[...] = jnp.zeros_like(st)
    along_z = [dev(0, 0, dz) for dz in FAR[:7]]
    along_xy = [dev(dx, dy, 0) for dx, dy in ((2, 1), (2, 0), (1, 1), (3, 1), (1, 0), (3, 0), (0, 1))]
    row_max, row_sum, row_teach = share(local_max, local_sum, teacher_sum, 0, st_z, along_z)
    row_max, row_sum, row_teach = share(row_max, row_sum, row_teach, 1, st_xy, along_xy)

    up = cot[...] * jnp.exp(local_max - row_max) / row_sum
    down = cot[...] / row_teach

    def grads(b, _):
        r = rows(b * 32, 32)
        g = (logits[r, :] * up - teach[r, :] * down).astype(BF)
        tg[r, :] = g
        tg_all[r, own_lanes] = g
        return 0

    lax.fori_loop(0, V // 32, grads, 0)

    remote(tg, tg_all.at[:, own_lanes], tg_send.at[0], tg_recv.at[0], opposite).start()
    remote(tg, tg_all.at[:, own_lanes], tg_send.at[1], tg_recv.at[1], twin).start()

    def dot_chunk(start):
        return lax.dot_general(
            w[:, rows(start, 512)], tg[...], (((0,), (0,)), ((), ())), preferred_element_type=F32
        )

    def far(dy, _):
        start = chunk(2, dy)
        part[rows(start, 512), :] = dot_chunk(start).astype(BF)
        for k in range(7):
            src = part.at[rows(start + (z + FAR[k]) % 8 * 64, 64), :]
            remote(src, rf.at[dy, k], rf_send.at[dy, k], rf_recv.at[dy, k], dev(0, 0, FAR[k])).start()
        return 0

    lax.fori_loop(0, 2, far, 0)

    def side(i, _):
        way, dy = i % 2, 1 - i // 2
        start = chunk(1 + 2 * way, dy)
        part[rows(start, 512), :] = dot_chunk(start).astype(BF)
        for k in range(8):
            zz = (z + FAR[k]) % 8
            src = part.at[rows(start + zz * 64, 64), :]
            dst = rx.at[way, dy, rows(zz * 64, 64), :]
            remote(src, dst, rs_send.at[way, dy, k], rs_recv.at[way, dy, k], dev(1 - 2 * way, 0, 0)).start()
        return 0

    lax.fori_loop(0, 4, side, 0)

    def own(dy, _):
        acc[dy] = dot_chunk(chunk(0, dy))
        return 0

    lax.fori_loop(0, 2, own, 0)

    def with_sides(dy, k, r):
        total = acc[dy, r, :]
        for way in range(2):
            arrived(rx.at[way, dy, r, :], rs_recv.at[way, dy, k])
            total += rx[way, dy, r, :].astype(F32)
        return total

    for k in range(8):
        r = rows((z + FAR[k]) % 8 * 64, 64)
        qy[r, :] = with_sides(1, k, r).astype(BF)
        remote(qy.at[r, :], ry.at[r, :], ry_send.at[k], ry_recv.at[k], dev(0, 1, 0)).start()
    for k in range(8):
        r = rows((z + FAR[k]) % 8 * 64, 64)
        total = with_sides(0, k, r)
        arrived(ry.at[r, :], ry_recv.at[k])
        total += ry[r, :].astype(F32)
        if k < 7:
            qz[r, :] = total.astype(BF)
            remote(qz.at[r, :], rz.at[k], rz_send.at[k], rz_recv.at[k], dev(0, 0, FAR[k])).start()
        else:
            acc[0, 0:64, :] = total

    for dy in range(2):
        total = part[rows(chunk(2, dy) + z * 64, 64), :].astype(F32)
        for k in range(7):
            arrived(rf.at[dy, k], rf_recv.at[dy, k])
            total += rf[dy, k].astype(F32)
        qf[dy] = total.astype(BF)
        remote(qf.at[dy], ro.at[dy], ro_send.at[dy], ro_recv.at[dy], dev(2, dy, 0)).start()

    arrived(tg_all.at[:, own_lanes], tg_recv.at[0])
    src = tg_all.at[:, rows((other + core) * T, T)]
    remote(src, src, tg_send.at[2], tg_recv.at[2], twin).start()
    arrived(tg_all.at[:, own_lanes], tg_recv.at[1])
    arrived(hx_all.at[:, own_lanes], hx_recv.at[2])
    for c2 in range(2):
        arrived(hx_all.at[rows(y * 512, 512), own_lanes], hx_recv.at[3 + c2])
    arrived(tg_all.at[:, own_lanes], tg_recv.at[2])

    def head(i, _):
        r = rows(i * 304, 304)
        head_out[r, :] = lax.dot_general(
            tg_all[r, :], hx_all[...], (((1,), (1,)), ((), ())), preferred_element_type=F32
        ).astype(BF)
        return 0

    lax.fori_loop(0, 4, head, 0)

    total = acc[0, 0:64, :]
    for k in range(7):
        arrived(rz.at[k], rz_recv.at[k])
        total += rz[k].astype(F32)
    for dy in range(2):
        arrived(ro.at[dy], ro_recv.at[dy])
        total += ro[dy].astype(F32)
    hg_out[...] = total.astype(BF)

    one = h.at[0:64, :]
    for k in range(8):
        for f in range(2):
            if k or not f:
                sent(one, ag_send_z.at[f, k])
            sent(one, ag_send_y.at[f, k])
            sent(one, ag_send_x.at[0, f, k])
            sent(one, ag_send_x.at[1, f, k])
            sent(one, rs_send.at[0, f, k])
            sent(one, rs_send.at[1, f, k])
            if k < 7:
                sent(one, rf_send.at[f, k])
        sent(one, ry_send.at[k])
        if k < 7:
            sent(one, rz_send.at[k])
    for i in range(2):
        sent(h.at[0:512, :], hx_send.at[i])
        sent(h.at[0:512, :], hx_send.at[3 + i])
        sent(one, ro_send.at[i])
        for j in range(7):
            sent(st.at[i], st_send.at[i, j])
    sent(h.at[0:1024, :], hx_send.at[2])
    for i in range(3):
        sent(tg, tg_send.at[i])


def per_device(hidden, head_weight, teacher_codes, teacher_scales, loss_cotangent):
    dma = pltpu.SemaphoreType.DMA
    vmem = pl.BlockSpec(memory_space=pltpu.VMEM)
    hbm = pl.BlockSpec(memory_space=pltpu.HBM)
    hidden_grad, head_grad = pl.pallas_call(
        kernel,
        name="head_backward",
        out_shape=(
            jax.ShapeDtypeStruct((64, T), BF),
            jax.ShapeDtypeStruct((V, 1024), BF),
        ),
        in_specs=[hbm] * 5,
        out_specs=(vmem, vmem),
        scratch_shapes=[
            pltpu.VMEM((38, T), jnp.int32),
            pltpu.VMEM((1, T), F32),
            pltpu.VMEM((4096, T), BF),
            pltpu.VMEM((V, 4096), BF),
            pltpu.VMEM((V, T), jnp.int32),
            pltpu.VMEM((V, T), F32),
            pltpu.VMEM((V, T), F32),
            pltpu.VMEM((V, T), BF),
            pltpu.VMEM((V, 4 * T), BF),
            pltpu.VMEM((1024, 4 * T), BF),
            pltpu.VMEM((4096, T), BF),
            pltpu.VMEM((2, 2, 512, T), BF),
            pltpu.VMEM((2, 7, 64, T), BF),
            pltpu.VMEM((2, 64, T), BF),
            pltpu.VMEM((2, 64, T), BF),
            pltpu.VMEM((2, 512, T), F32),
            pltpu.VMEM((512, T), BF),
            pltpu.VMEM((512, T), BF),
            pltpu.VMEM((512, T), BF),
            pltpu.VMEM((7, 64, T), BF),
            pltpu.VMEM((2, 8, T), F32),
            pltpu.VMEM((7, 8, T), F32),
            pltpu.VMEM((7, 8, T), F32),
            dma((6,)),
            dma((2, 8)),
            dma((2, 8)),
            dma((2, 2, 8)),
            dma((4, 2, 8)),
            dma((5,)),
            dma((5,)),
            dma((3,)),
            dma((3,)),
            dma((2, 7)),
            dma((2, 7)),
            dma((2, 2, 8)),
            dma((2, 2, 8)),
            dma((2, 7)),
            dma((2, 7)),
            dma((2,)),
            dma((2,)),
            dma((8,)),
            dma((8,)),
            dma((7,)),
            dma((7,)),
        ],
        compiler_params=pltpu.CompilerParams(
            collective_id=0, has_side_effects=True, vmem_limit_bytes=48 << 20
        ),
        cost_estimate=pl.CostEstimate(
            flops=6 * V * T * 4096, bytes_accessed=14 << 20, transcendentals=2 * V * T
        ),
    )(*(
        pltpu.with_memory_space_constraint(a, pltpu.HBM)
        for a in (hidden.T, teacher_scales.T, loss_cotangent.reshape(1, T), head_weight, teacher_codes.T)
    ))
    return hidden_grad.T, head_grad


def solution(mesh):
    return jax.shard_map(
        per_device,
        mesh=mesh,
        in_specs=(P("dp", "vocab"), P("vocab", None), P("dp", "vocab"), P("dp", "vocab"), P("dp")),
        out_specs=(P("dp", "vocab"), P("vocab", "dp")),
        check_vma=False,
    )
```

time: 90.4 us -> 78.1 us (0.86)
  the two profiles are of different devices: /device:TPU:37 before, /device:TPU:5 now
where the time goes in v2:
time: 78.1 us; the launch traced here: 76.5 us
  Pallas kernels  73.8 us (94%)
  local copies, waits for them, and re-layouts  2.07 us (3%)
    pallas_call x1, Pallas kernels, per_device(): pl.pallas_call(kernel, name='head_backward', out_shape=(jax.ShapeDtypeStr...  73.8 us
    unnamed x2, local copies, waits for them, and re-layouts  2.07 us

profile of v2, /device:TPU:5, one launch (start us, length us, event | category | flops | bytes accessed | tf_op | source)
XLA Modules:
  0.0 76.5 jit_solution(15218236746830873100)
XLA Ops:
  0.6 73.8 %head_backward.1 = (bf16[64,256]{1,0:T(8,128)(2,1)S(1)}, bf16[1216,1024]{1,0:T(8,128)(2,1)S(1)}) custom-call(bf16[64,256]{1,0:T(8,128)(2,1)} %bitcast.8, s32[38,256]{1,0:T(8,128)} %bitcast.7, f32[1,256]{1,0:T(1,128)} %bitcast.9, bf16[1216,4096]{1,0:T(8,128)(2,1)} %w_hbm.1, s32[1216,256]{1,0:T(8,128)} %bitcast.6), custom_call_target="tpu_custom_call" | custom-call | flops 7650410496 | bytes 14680064 | tf_op jit(solution)/shard_map/head_backward/pallas_call | solution.py:420
  74.5 0.6 copy.9
  75.1 1.4 %copy.10 = bf16[1216,1024]{1,0:T(8,128)(2,1)} copy(bf16[1216,1024]{1,0:T(8,128)(2,1)S(1)} %get-tuple-element.9) | data formatting | bytes 4980736

commit v3 on v2

--- a/solution.py
+++ b/solution.py
@@ -11,6 +11,7 @@
 
 V = 1216
 T = 256
+EARLY = 4
 NEAR = (0, 1, 7, 2, 6, 3, 5, 4)
 FAR = (4, 3, 5, 2, 6, 1, 7, 0)
 
@@ -164,16 +165,16 @@
 
     own_lanes = rows(d * T, T)
 
-    def hidden_across(dx):
+    def hidden_across(dx, dy):
         quarter = (x + dx) % 4
 
         @pl.when(quarter // 2 == 1 - yh)
         def _():
             c2 = quarter % 2
-            src = h.at[rows(chunk(dx, 0), 512), :]
-            dst = hx_all.at[rows(y * 512, 512), own_lanes]
+            src = h.at[rows(chunk(dx, dy), 512), :]
+            dst = hx_all.at[rows((y + dy) % 2 * 512, 512), own_lanes]
             to = (at(0, 1, 0), other + c2)
-            remote(src, dst, hx_send.at[c2], hx_recv.at[core], to).start()
+            remote(src, dst, hx_send.at[c2, dy], hx_recv.at[core, dy], to).start()
 
     pass_on(block(0, 0, 0), ag_send_z.at[0, 0], ag_recv.at[1, 0, 0], dev(2, 0, 0))
     spread_z(0)
@@ -187,14 +188,15 @@
             arrived(block(2, 0, 0), ag_recv.at[1, 0, 0])
             spread_z(1)
             spread_y(1, 0)
-    hidden_across(0)
+    hidden_across(0, 0)
     for k in range(8):
         arrived(block(0, 1, k), ag_recv.at[0, 1, k])
         spread_x(1, k)
         if k:
             arrived(block(2, 0, k), ag_recv.at[1, 0, k])
             spread_y(1, k)
-    hidden_across(2)
+    hidden_across(0, 1)
+    hidden_across(2, 0)
 
     def add_logits(start):
         f = rows(start, 512)
@@ -213,9 +215,9 @@
         for k in range(8):
             for i, dx in ((0, 1), (1, -1)):
                 arrived(block(-dx, dy, k), ag_recv.at[2 + i, dy, k])
+        hidden_across(1, dy)
+        hidden_across(3, dy)
         if dy == 0:
-            hidden_across(1)
-            hidden_across(3)
 
             def dots_side(i, _):
                 add_logits(chunk(1 + 2 * i, 0))
@@ -224,8 +226,9 @@
             lax.fori_loop(0, 2, dots_side, 0)
     for k in range(8):
         arrived(block(2, 1, k), ag_recv.at[1, 1, k])
+    hidden_across(2, 1)
     src = h.at[rows((yh * 2 + 1 - core) * 1024, 1024), :]
-    remote(src, hx_all.at[:, own_lanes], hx_send.at[2], hx_recv.at[2], twin).start()
+    remote(src, hx_all.at[:, own_lanes], hx_send.at[2, 0], hx_recv.at[2, 0], twin).start()
     hx_all[:, own_lanes] = h[rows(d * 1024, 1024), :]
 
     def dots_last(i, _):
@@ -249,31 +252,23 @@
     s = lax.fori_loop(0, V // 32, exps, jnp.zeros((32, T), F32))
     local_sum = jnp.sum(s, axis=0, keepdims=True)
 
-    def hidden_along():
-        for c2 in range(2):
-            lanes = rows((other + c2) * T, T)
-            src = hx_all.at[rows((1 - y) * 512, 512), lanes]
-            arrived(src, hx_recv.at[c2])
-            remote(src, src, hx_send.at[3 + c2], hx_recv.at[3 + c2], dev(0, 1, 0)).start()
-
     def share(m, s, t, stage, buf, peers):
-        st[stage, 0:1, :] = m
-        st[stage, 1:2, :] = s
-        st[stage, 2:3, :] = t
+        for n, value in enumerate((m, s, t)):
+            for half in range(2):
+                st[stage, 2 * n + half : 2 * n + half + 1, :] = value[:, half * 128 : half * 128 + 128]
         for j, p in enumerate(peers):
             remote(st.at[stage], buf.at[j], st_send.at[stage, j], st_recv.at[stage, j], p).start()
-        if stage:
-            hidden_along()
         for j in range(7):
             arrived(buf.at[j], st_recv.at[stage, j])
+        m, s, t = (st[stage, 2 * n : 2 * n + 2, :] for n in range(3))
         best = m
         for j in range(7):
-            best = jnp.maximum(best, buf[j, 0:1, :])
+            best = jnp.maximum(best, buf[j, 0:2, :])
         s = s * jnp.exp(m - best)
         for j in range(7):
-            s += buf[j, 1:2, :] * jnp.exp(buf[j, 0:1, :] - best)
-            t += buf[j, 2:3, :]
-        return best, s, t
+            s += buf[j, 2:4, :] * jnp.exp(buf[j, 0:2, :] - best)
+            t += buf[j, 4:6, :]
+        return tuple(jnp.concatenate([a[0:1, :], a[1:2, :]], axis=1) for a in (best, s, t))
 
     st[...] = jnp.zeros_like(st)
     along_z = [dev(0, 0, dz) for dz in FAR[:7]]
@@ -293,8 +288,16 @@
 
     lax.fori_loop(0, V // 32, grads, 0)
 
-    remote(tg, tg_all.at[:, own_lanes], tg_send.at[0], tg_recv.at[0], opposite).start()
-    remote(tg, tg_all.at[:, own_lanes], tg_send.at[1], tg_recv.at[1], twin).start()
+    def tile(i):
+        return rows(i * 304, 304)
+
+    def tokens_across(i):
+        dst = tg_all.at[tile(i), own_lanes]
+        remote(tg.at[tile(i), :], dst, tg_send.at[i], tg_recv.at[i], opposite).start()
+
+    for i in range(EARLY):
+        tokens_across(i)
+    remote(tg, tg_all.at[:, own_lanes], tg_send.at[8], tg_recv.at[8], twin).start()
 
     def dot_chunk(start):
         return lax.dot_general(
@@ -341,6 +344,8 @@
         r = rows((z + FAR[k]) % 8 * 64, 64)
         qy[r, :] = with_sides(1, k, r).astype(BF)
         remote(qy.at[r, :], ry.at[r, :], ry_send.at[k], ry_recv.at[k], dev(0, 1, 0)).start()
+    for i in range(EARLY, 4):
+        tokens_across(i)
     for k in range(8):
         r = rows((z + FAR[k]) % 8 * 64, 64)
         total = with_sides(0, k, r)
@@ -360,23 +365,30 @@
         qf[dy] = total.astype(BF)
         remote(qf.at[dy], ro.at[dy], ro_send.at[dy], ro_recv.at[dy], dev(2, dy, 0)).start()
 
-    arrived(tg_all.at[:, own_lanes], tg_recv.at[0])
-    src = tg_all.at[:, rows((other + core) * T, T)]
-    remote(src, src, tg_send.at[2], tg_recv.at[2], twin).start()
-    arrived(tg_all.at[:, own_lanes], tg_recv.at[1])
-    arrived(hx_all.at[:, own_lanes], hx_recv.at[2])
+    def head(i):
+        arrived(tg_all.at[tile(i), own_lanes], tg_recv.at[4 + i])
+        head_out[tile(i), :] = lax.dot_general(
+            tg_all[tile(i), :], hx_all[...], (((1,), (1,)), ((), ())), preferred_element_type=F32
+        ).astype(BF)
+
+    def head_step(i, _):
+        src = tg_all.at[tile(i), rows((other + core) * T, T)]
+        arrived(src, tg_recv.at[i])
+        remote(src, src, tg_send.at[4 + i], tg_recv.at[4 + i], twin).start()
+
+        @pl.when(i > 0)
+        def _():
+            head(i - 1)
+
+        return 0
+
+    arrived(hx_all.at[:, own_lanes], hx_recv.at[2, 0])
     for c2 in range(2):
-        arrived(hx_all.at[rows(y * 512, 512), own_lanes], hx_recv.at[3 + c2])
-    arrived(tg_all.at[:, own_lanes], tg_recv.at[2])
-
-    def head(i, _):
-        r = rows(i * 304, 304)
-        head_out[r, :] = lax.dot_general(
-            tg_all[r, :], hx_all[...], (((1,), (1,)), ((), ())), preferred_element_type=F32
-        ).astype(BF)
-        return 0
-
-    lax.fori_loop(0, 4, head, 0)
+        for dy in range(2):
+            arrived(hx_all.at[0:512, own_lanes], hx_recv.at[c2, dy])
+    arrived(tg_all.at[:, own_lanes], tg_recv.at[8])
+    lax.fori_loop(0, 4, head_step, 0)
+    head(3)
 
     total = acc[0, 0:64, :]
     for k in range(7):
@@ -403,14 +415,15 @@
         if k < 7:
             sent(one, rz_send.at[k])
     for i in range(2):
-        sent(h.at[0:512, :], hx_send.at[i])
-        sent(h.at[0:512, :], hx_send.at[3 + i])
+        for dy in range(2):
+            sent(h.at[0:512, :], hx_send.at[i, dy])
         sent(one, ro_send.at[i])
         for j in range(7):
             sent(st.at[i], st_send.at[i, j])
-    sent(h.at[0:1024, :], hx_send.at[2])
-    for i in range(3):
-        sent(tg, tg_send.at[i])
+    sent(h.at[0:1024, :], hx_send.at[2, 0])
+    for i in range(8):
+        sent(tg.at[0:304, :], tg_send.at[i])
+    sent(tg, tg_send.at[8])
 
 
 def per_device(hidden, head_weight, teacher_codes, teacher_scales, loss_cotangent):
@@ -447,18 +460,18 @@
             pltpu.VMEM((512, T), BF),
             pltpu.VMEM((512, T), BF),
             pltpu.VMEM((7, 64, T), BF),
-            pltpu.VMEM((2, 8, T), F32),
-            pltpu.VMEM((7, 8, T), F32),
-            pltpu.VMEM((7, 8, T), F32),
+            pltpu.VMEM((2, 8, 128), F32),
+            pltpu.VMEM((7, 8, 128), F32),
+            pltpu.VMEM((7, 8, 128), F32),
             dma((6,)),
             dma((2, 8)),
             dma((2, 8)),
             dma((2, 2, 8)),
             dma((4, 2, 8)),
-            dma((5,)),
-            dma((5,)),
-            dma((3,)),
-            dma((3,)),
+            dma((3, 2)),
+            dma((3, 2)),
+            dma((9,)),
+            dma((9,)),
             dma((2, 7)),
             dma((2, 7)),
             dma((2, 2, 8)),

time: 78.1 us -> 69.3 us (0.89); the launches traced: 76.5 us -> 68.6 us
  Pallas kernels: 73.8 us -> 65.9 us
    pallas_call x1, Pallas kernels: 73.8 us -> 65.9 us  [per_device(): pl.pallas_call(kernel, name='head_backward', out_shape=(jax.ShapeDtypeStr...]
where the time goes in v3:
time: 69.3 us; the launch traced here: 68.6 us
  Pallas kernels  65.9 us (95%)
  local copies, waits for them, and re-layouts  2.07 us (3%)
    pallas_call x1, Pallas kernels, per_device(): pl.pallas_call(kernel, name='head_backward', out_shape=(jax.ShapeDtypeStr...  65.9 us
    unnamed x2, local copies, waits for them, and re-layouts  2.07 us

profile of v3, /device:TPU:5, one launch (start us, length us, event | category | flops | bytes accessed | tf_op | source)
XLA Modules:
  0.0 68.6 jit_solution(12554345648335323515)
XLA Ops:
  0.6 65.9 %head_backward.1 = (bf16[64,256]{1,0:T(8,128)(2,1)S(1)}, bf16[1216,1024]{1,0:T(8,128)(2,1)S(1)}) custom-call(bf16[64,256]{1,0:T(8,128)(2,1)} %bitcast.8, s32[38,256]{1,0:T(8,128)} %bitcast.7, f32[1,256]{1,0:T(1,128)} %bitcast.9, bf16[1216,4096]{1,0:T(8,128)(2,1)} %w_hbm.1, s32[1216,256]{1,0:T(8,128)} %bitcast.6), custom_call_target="tpu_custom_call" | custom-call | flops 7650410496 | bytes 14680064 | tf_op jit(solution)/shard_map/head_backward/pallas_call | solution.py:433
  66.6 0.6 copy.9
  67.2 1.4 %copy.10 = bf16[1216,1024]{1,0:T(8,128)(2,1)} copy(bf16[1216,1024]{1,0:T(8,128)(2,1)S(1)} %get-tuple-element.9) | data formatting | bytes 4980736

commit v4 on v3

--- a/solution.py
+++ b/solution.py
@@ -11,7 +11,6 @@
 
 V = 1216
 T = 256
-EARLY = 4
 NEAR = (0, 1, 7, 2, 6, 3, 5, 4)
 FAR = (4, 3, 5, 2, 6, 1, 7, 0)
 
@@ -40,14 +39,11 @@
     hx_all,
     part,
     rx,
-    rf,
-    qf,
+    rz,
+    qz,
+    qo,
     ro,
     acc,
-    qy,
-    ry,
-    qz,
-    rz,
     st,
     st_z,
     st_xy,
@@ -64,19 +60,16 @@
     st_recv,
     rs_send,
     rs_recv,
-    rf_send,
-    rf_recv,
+    rz_send,
+    rz_recv,
     ro_send,
     ro_recv,
-    ry_send,
-    ry_recv,
-    rz_send,
-    rz_recv,
 ):
     v = lax.axis_index("vocab")
     d = lax.axis_index("dp")
     x, y, z = v // 16, (v // 8) % 2, v % 8
     yh, core = d // 2, d % 2
+    turn = 1 - 2 * core
 
     def at(dx, dy, dz):
         return ((x + dx) % 4 * 2 + (y + dy) % 2) * 8 + (z + dz) % 8
@@ -157,8 +150,14 @@
         pass_on(block(2 * far, 0, k), ag_send_y.at[far, k], ag_recv.at[far, 1, k], dev(0, 1, 0))
 
     def spread_z(far):
-        for k in range(1, 8):
+        for k in (3, 4, 1, 2):
             pass_on(block(2 * far, 0, 0), ag_send_z.at[far, k], ag_recv.at[far, 0, k], dev(0, 0, NEAR[k]))
+
+    def forward_z(far):
+        for k, dz in ((3, 1), (4, -1)):
+            pass_on(block(2 * far, 0, k), ag_send_z.at[far, k + 2], ag_recv.at[far, 0, k + 2], dev(0, 0, dz))
+        b = h.at[rows(at(2 * far, 0, -2 * turn) * 64, 64), :]
+        pass_on(b, ag_send_z.at[far, 7], ag_recv.at[far, 0, 7], dev(0, 0, 2 * turn))
 
     def chunk(dx, dy):
         return ((x + dx) % 4 * 2 + (y + dy) % 2) * 512
@@ -180,22 +179,46 @@
     spread_z(0)
     spread_x(0, 0)
     spread_y(0, 0)
-    for k in range(1, 8):
+    def from_z(k):
         arrived(block(0, 0, k), ag_recv.at[0, 0, k])
+        if k == 4:
+            forward_z(0)
         spread_x(0, k)
         spread_y(0, k)
-        if k == 2:
-            arrived(block(2, 0, 0), ag_recv.at[1, 0, 0])
-            spread_z(1)
-            spread_y(1, 0)
-    hidden_across(0, 0)
-    for k in range(8):
+
+    def from_y(k):
         arrived(block(0, 1, k), ag_recv.at[0, 1, k])
         spread_x(1, k)
-        if k:
-            arrived(block(2, 0, k), ag_recv.at[1, 0, k])
-            spread_y(1, k)
-    hidden_across(0, 1)
+
+    def from_far(k):
+        arrived(block(2, 0, k), ag_recv.at[1, 0, k])
+        if k == 0:
+            spread_z(1)
+        if k == 4:
+            forward_z(1)
+        spread_y(1, k)
+
+    for step, ks in (
+        (from_z, (1, 2)),
+        (from_y, (0,)),
+        (from_z, (3, 4)),
+        (from_far, (0,)),
+        (from_y, (1, 2)),
+        (from_z, (5, 6)),
+        (from_y, (3, 4)),
+        (from_z, (7,)),
+        (from_far, (3, 4)),
+        (from_y, (5, 6)),
+        (from_far, (1, 2)),
+        (from_y, (7,)),
+        (from_far, (5, 6, 7)),
+    ):
+        for k in ks:
+            step(k)
+        if step is from_z and 7 in ks:
+            hidden_across(0, 0)
+        if step is from_y and 7 in ks:
+            hidden_across(0, 1)
     hidden_across(2, 0)
 
     def add_logits(start):
@@ -279,6 +302,13 @@
     up = cot[...] * jnp.exp(local_max - row_max) / row_sum
     down = cot[...] / row_teach
 
+    def tile(i):
+        return rows(i * 304, 304)
+
+    def tokens_across(i):
+        dst = tg_all.at[tile(i), own_lanes]
+        remote(tg.at[tile(i), :], dst, tg_send.at[i], tg_recv.at[i], opposite).start()
+
     def grads(b, _):
         r = rows(b * 32, 32)
         g = (logits[r, :] * up - teach[r, :] * down).astype(BF)
@@ -286,16 +316,8 @@
         tg_all[r, own_lanes] = g
         return 0
 
-    lax.fori_loop(0, V // 32, grads, 0)
-
-    def tile(i):
-        return rows(i * 304, 304)
-
-    def tokens_across(i):
-        dst = tg_all.at[tile(i), own_lanes]
-        remote(tg.at[tile(i), :], dst, tg_send.at[i], tg_recv.at[i], opposite).start()
-
-    for i in range(EARLY):
+    for i, (lo, hi) in enumerate(((0, 10), (10, 19), (19, 29), (29, 38))):
+        lax.fori_loop(lo, hi, grads, 0)
         tokens_across(i)
     remote(tg, tg_all.at[:, own_lanes], tg_send.at[8], tg_recv.at[8], twin).start()
 
@@ -304,18 +326,33 @@
             w[:, rows(start, 512)], tg[...], (((0,), (0,)), ((), ())), preferred_element_type=F32
         )
 
-    def far(dy, _):
-        start = chunk(2, dy)
-        part[rows(start, 512), :] = dot_chunk(start).astype(BF)
-        for k in range(7):
-            src = part.at[rows(start + (z + FAR[k]) % 8 * 64, 64), :]
-            remote(src, rf.at[dy, k], rf_send.at[dy, k], rf_recv.at[dy, k], dev(0, 0, FAR[k])).start()
-        return 0
-
-    lax.fori_loop(0, 2, far, 0)
-
-    def side(i, _):
-        way, dy = i % 2, 1 - i // 2
+    def along_z(plane, dy, slot, src, dz):
+        ss, rs = rz_send.at[plane, dy, slot], rz_recv.at[plane, dy, slot]
+        remote(src, rz.at[plane, dy, slot], ss, rs, dev(0, 0, dz)).start()
+
+    def came(plane, dy, slot):
+        arrived(rz.at[plane, dy, slot], rz_recv.at[plane, dy, slot])
+        return rz[plane, dy, slot].astype(F32)
+
+    def two_away(plane, dy, mine):
+        for i in range(2):
+            a = (core + i) % 2
+            dz = 2 - 4 * a
+            total = mine(dz) + came(plane, dy, 1 + a)
+            if i == 0:
+                total += came(plane, dy, 0)
+            qz[plane, dy, 3 + i] = total.astype(BF)
+            along_z(plane, dy, 3 + a, qz.at[plane, dy, 3 + i], dz)
+
+    def over_z(plane, dy, mine):
+        total = mine(0)
+        for slot in range(3, 7):
+            total += came(plane, dy, slot)
+        return total
+
+    straight = ((4, 0, 2 * turn), (3, 1, 1), (-3, 2, -1), (1, 5, 1), (-1, 6, -1))
+
+    def side(way, dy):
         start = chunk(1 + 2 * way, dy)
         part[rows(start, 512), :] = dot_chunk(start).astype(BF)
         for k in range(8):
@@ -323,47 +360,72 @@
             src = part.at[rows(start + zz * 64, 64), :]
             dst = rx.at[way, dy, rows(zz * 64, 64), :]
             remote(src, dst, rs_send.at[way, dy, k], rs_recv.at[way, dy, k], dev(1 - 2 * way, 0, 0)).start()
+
+    def far(dy):
+        start = chunk(2, dy)
+        part[rows(start, 512), :] = dot_chunk(start).astype(BF)
+        for dz, slot, to in straight:
+            along_z(0, dy, slot, part.at[rows(start + (z + dz) % 8 * 64, 64), :], to)
+
+    def dots(i, _):
+        @pl.when((i == 0) | (i == 3))
+        def _():
+            far(1 - i // 3)
+
+        @pl.when((i == 1) | (i == 2))
+        def _():
+            side(i - 1, 1)
+
+        @pl.when((i == 4) | (i == 5))
+        def _():
+            side(i - 4, 0)
+
+        @pl.when(i > 5)
+        def _():
+            acc[7 - i] = dot_chunk(chunk(0, 7 - i))
+
         return 0
 
-    lax.fori_loop(0, 4, side, 0)
-
-    def own(dy, _):
-        acc[dy] = dot_chunk(chunk(0, dy))
-        return 0
-
-    lax.fori_loop(0, 2, own, 0)
-
-    def with_sides(dy, k, r):
+    lax.fori_loop(0, 8, dots, 0)
+
+    def far_block(dy):
+        return lambda dz: part[rows(chunk(2, dy) + (z + dz) % 8 * 64, 64), :].astype(F32)
+
+    def near_block(dy):
+        return lambda dz: acc[dy, rows((z + dz) % 8 * 64, 64), :]
+
+    def with_sides(dy, k):
+        r = rows((z + FAR[k]) % 8 * 64, 64)
         total = acc[dy, r, :]
         for way in range(2):
             arrived(rx.at[way, dy, r, :], rs_recv.at[way, dy, k])
             total += rx[way, dy, r, :].astype(F32)
-        return total
-
-    for k in range(8):
-        r = rows((z + FAR[k]) % 8 * 64, 64)
-        qy[r, :] = with_sides(1, k, r).astype(BF)
-        remote(qy.at[r, :], ry.at[r, :], ry_send.at[k], ry_recv.at[k], dev(0, 1, 0)).start()
-    for i in range(EARLY, 4):
-        tokens_across(i)
-    for k in range(8):
-        r = rows((z + FAR[k]) % 8 * 64, 64)
-        total = with_sides(0, k, r)
-        arrived(ry.at[r, :], ry_recv.at[k])
-        total += ry[r, :].astype(F32)
-        if k < 7:
-            qz[r, :] = total.astype(BF)
-            remote(qz.at[r, :], rz.at[k], rz_send.at[k], rz_recv.at[k], dev(0, 0, FAR[k])).start()
-        else:
-            acc[0, 0:64, :] = total
-
-    for dy in range(2):
-        total = part[rows(chunk(2, dy) + z * 64, 64), :].astype(F32)
-        for k in range(7):
-            arrived(rf.at[dy, k], rf_recv.at[dy, k])
-            total += rf[dy, k].astype(F32)
-        qf[dy] = total.astype(BF)
-        remote(qf.at[dy], ro.at[dy], ro_send.at[dy], ro_recv.at[dy], dev(2, dy, 0)).start()
+        return r, total
+
+    def near(dy, ks):
+        for k in ks:
+            r, total = with_sides(dy, k)
+            acc[dy, r, :] = total
+            for dz, slot, to in straight:
+                if dz % 8 == FAR[k]:
+                    qz[1, dy, slot] = total.astype(BF)
+                    along_z(1, dy, slot, qz.at[1, dy, slot], to)
+
+    def give(i, total, to):
+        qo[i] = total.astype(BF)
+        remote(qo.at[i], ro.at[i], ro_send.at[i], ro_recv.at[i], to).start()
+
+    def to_twin(i):
+        src = tg_all.at[tile(i), rows((other + core) * T, T)]
+        arrived(src, tg_recv.at[i])
+        remote(src, src, tg_send.at[4 + i], tg_recv.at[4 + i], twin).start()
+
+    def hidden_here():
+        arrived(hx_all.at[:, own_lanes], hx_recv.at[2, 0])
+        for c2 in range(2):
+            for dy in range(2):
+                arrived(hx_all.at[0:512, own_lanes], hx_recv.at[c2, dy])
+        arrived(tg_all.at[:, own_lanes], tg_recv.at[8])
 
     def head(i):
         arrived(tg_all.at[tile(i), own_lanes], tg_recv.at[4 + i])
@@ -371,32 +433,33 @@
             tg_all[tile(i), :], hx_all[...], (((1,), (1,)), ((), ())), preferred_element_type=F32
         ).astype(BF)
 
-    def head_step(i, _):
-        src = tg_all.at[tile(i), rows((other + core) * T, T)]
-        arrived(src, tg_recv.at[i])
-        remote(src, src, tg_send.at[4 + i], tg_recv.at[4 + i], twin).start()
-
-        @pl.when(i > 0)
-        def _():
-            head(i - 1)
-
-        return 0
-
-    arrived(hx_all.at[:, own_lanes], hx_recv.at[2, 0])
-    for c2 in range(2):
-        for dy in range(2):
-            arrived(hx_all.at[0:512, own_lanes], hx_recv.at[c2, dy])
-    arrived(tg_all.at[:, own_lanes], tg_recv.at[8])
-    lax.fori_loop(0, 4, head_step, 0)
+    two_away(0, 1, far_block(1))
+    near(1, (0, 1, 2))
+    two_away(0, 0, far_block(0))
+    near(1, (3, 4, 5, 6))
+    two_away(1, 1, near_block(1))
+    near(1, (7,))
+    for dy in (1, 0):
+        give(dy, over_z(0, dy, far_block(dy)), dev(2, dy, 0))
+    near(0, (0, 1, 2, 3))
+    give(2, over_z(1, 1, near_block(1)), dev(0, 1, 0))
+    near(0, (4, 5))
+    to_twin(0)
+    two_away(1, 0, near_block(0))
+    to_twin(1)
+    hidden_here()
+    head(0)
+    near(0, (6, 7))
+    to_twin(2)
+    head(1)
+    to_twin(3)
+    head(2)
     head(3)
 
-    total = acc[0, 0:64, :]
-    for k in range(7):
-        arrived(rz.at[k], rz_recv.at[k])
-        total += rz[k].astype(F32)
-    for dy in range(2):
-        arrived(ro.at[dy], ro_recv.at[dy])
-        total += ro[dy].astype(F32)
+    total = over_z(1, 0, near_block(0))
+    for i in range(3):
+        arrived(ro.at[i], ro_recv.at[i])
+        total += ro[i].astype(F32)
     hg_out[...] = total.astype(BF)
 
     one = h.at[0:64, :]
@@ -410,14 +473,13 @@
             sent(one, rs_send.at[0, f, k])
             sent(one, rs_send.at[1, f, k])
             if k < 7:
-                sent(one, rf_send.at[f, k])
-        sent(one, ry_send.at[k])
-        if k < 7:
-            sent(one, rz_send.at[k])
+                for dy in range(2):
+                    sent(one, rz_send.at[f, dy, k])
+    for i in range(3):
+        sent(one, ro_send.at[i])
     for i in range(2):
         for dy in range(2):
             sent(h.at[0:512, :], hx_send.at[i, dy])
-        sent(one, ro_send.at[i])
         for j in range(7):
             sent(st.at[i], st_send.at[i, j])
     sent(h.at[0:1024, :], hx_send.at[2, 0])
@@ -452,14 +514,11 @@
             pltpu.VMEM((1024, 4 * T), BF),
             pltpu.VMEM((4096, T), BF),
             pltpu.VMEM((2, 2, 512, T), BF),
-            pltpu.VMEM((2, 7, 64, T), BF),
-            pltpu.VMEM((2, 64, T), BF),
-            pltpu.VMEM((2, 64, T), BF),
+            pltpu.VMEM((2, 2, 7, 64, T), BF),
+            pltpu.VMEM((2, 2, 7, 64, T), BF),
+            pltpu.VMEM((3, 64, T), BF),
+            pltpu.VMEM((3, 64, T), BF),
             pltpu.VMEM((2, 512, T), F32),
-            pltpu.VMEM((512, T), BF),
-            pltpu.VMEM((512, T), BF),
-            pltpu.VMEM((512, T), BF),
-            pltpu.VMEM((7, 64, T), BF),
             pltpu.VMEM((2, 8, 128), F32),
             pltpu.VMEM((7, 8, 128), F32),
             pltpu.VMEM((7, 8, 128), F32),
@@ -476,14 +535,10 @@
             dma((2, 7)),
             dma((2, 2, 8)),
             dma((2, 2, 8)),
-            dma((2, 7)),
-            dma((2, 7)),
-            dma((2,)),
-            dma((2,)),
-            dma((8,)),
-            dma((8,)),
-            dma((7,)),
-            dma((7,)),
+            dma((2, 2, 7)),
+            dma((2, 2, 7)),
+            dma((3,)),
+            dma((3,)),
         ],
         compiler_params=pltpu.CompilerParams(
             collective_id=0, has_side_effects=True, vmem_limit_bytes=48 << 20

time: 69.3 us -> 67.5 us (0.974)
  Pallas kernels: 65.9 us -> 64.8 us
    pallas_call x1, Pallas kernels: 65.9 us -> 64.8 us  [per_device(): pl.pallas_call(kernel, name='head_backward', out_shape=(jax.ShapeDtypeStr...]
where the time goes in v4:
time: 67.5 us
  Pallas kernels  64.8 us (96%)
  local copies, waits for them, and re-layouts  2.07 us (3%)
    pallas_call x1, Pallas kernels, per_device(): pl.pallas_call(kernel, name='head_backward', out_shape=(jax.ShapeDtypeStr...  64.8 us
    unnamed x2, local copies, waits for them, and re-layouts  2.07 us

profile of v4, /device:TPU:5, one launch (start us, length us, event | category | flops | bytes accessed | tf_op | source)
XLA Modules:
  0.0 67.5 jit_solution(10206048483276961054)
XLA Ops:
  0.6 64.8 %head_backward.1 = (bf16[64,256]{1,0:T(8,128)(2,1)S(1)}, bf16[1216,1024]{1,0:T(8,128)(2,1)S(1)}) custom-call(bf16[64,256]{1,0:T(8,128)(2,1)} %bitcast.8, s32[38,256]{1,0:T(8,128)} %bitcast.7, f32[1,256]{1,0:T(1,128)} %bitcast.9, bf16[1216,4096]{1,0:T(8,128)(2,1)} %w_hbm.1, s32[1216,256]{1,0:T(8,128)} %bitcast.6), custom_call_target="tpu_custom_call" | custom-call | flops 7650410496 | bytes 14680064 | tf_op jit(solution)/shard_map/head_backward/pallas_call | solution.py:495
  65.4 0.6 copy.9
  66.0 1.4 %copy.10 = bf16[1216,1024]{1,0:T(8,128)(2,1)} copy(bf16[1216,1024]{1,0:T(8,128)(2,1)S(1)} %get-tuple-element.9) | data formatting | bytes 4980736

commit v5 on v4

--- a/solution.py
+++ b/solution.py
@@ -451,8 +451,8 @@
     head(0)
     near(0, (6, 7))
     to_twin(2)
+    to_twin(3)
     head(1)
-    to_twin(3)
     head(2)
     head(3)
 

time: 67.5 us -> 67.5 us (level)
  no operation moved by 1% of the time
where the time goes in v5:
time: 67.5 us; the launch traced here: 67.4 us
  Pallas kernels  64.7 us (96%)
  local copies, waits for them, and re-layouts  2.07 us (3%)
    pallas_call x1, Pallas kernels, per_device(): pl.pallas_call(kernel, name='head_backward', out_shape=(jax.ShapeDtypeStr...  64.7 us
    unnamed x2, local copies, waits for them, and re-layouts  2.07 us

profile of v5, /device:TPU:5, one launch (start us, length us, event | category | flops | bytes accessed | tf_op | source)
XLA Modules:
  0.0 67.4 jit_solution(4280088250683841663)
XLA Ops:
  0.6 64.7 %head_backward.1 = (bf16[64,256]{1,0:T(8,128)(2,1)S(1)}, bf16[1216,1024]{1,0:T(8,128)(2,1)S(1)}) custom-call(bf16[64,256]{1,0:T(8,128)(2,1)} %bitcast.8, s32[38,256]{1,0:T(8,128)} %bitcast.7, f32[1,256]{1,0:T(1,128)} %bitcast.9, bf16[1216,4096]{1,0:T(8,128)(2,1)} %w_hbm.1, s32[1216,256]{1,0:T(8,128)} %bitcast.6), custom_call_target="tpu_custom_call" | custom-call | flops 7650410496 | bytes 14680064 | tf_op jit(solution)/shard_map/head_backward/pallas_call | solution.py:495
  65.4 0.6 copy.9
  66.0 1.4 %copy.10 = bf16[1216,1024]{1,0:T(8,128)(2,1)} copy(bf16[1216,1024]{1,0:T(8,128)(2,1)S(1)} %get-tuple-element.9) | data formatting | bytes 4980736
